TPU v7x, 32 devices: a whole 2x2x4 slice. The times are simulated.
32 devices in a mesh: frag: 4 (over y, x), orb: 8 (over z, core).
Axes of the slice: x: 2, y: 2, z: 4, core: 2. Of those that a mesh axis runs over, the one named last changes fastest.
Arguments:
- orbitals: float32 [8, 128, 48, 2304], P('frag', 'orb'), may hold values from -6 to 6
- potential: float32 [24, 36864], P('frag', 'orb'), may hold values from -3 to 0
- ion_potential: float32 [24, 36864], P('frag', 'orb'), may hold values from -2 to 0
- core_density: float32 [24, 36864], P('frag', 'orb'), may hold values from 0.5 to 2
- frag_blocks: int32 [8, 3], replicated, may hold values from 0 to 23, as said below
- frag_signs: int32 [8], replicated, may hold values from -1 to 1, as said below
Outputs:
- filtered: float32 [8, 128, 48, 2304], P('frag', 'orb')
- new_potential: float32 [24, 36864], P('frag', 'orb')
Inputs may be any that keep to these rules, and one draw needn't show every extreme that they name: `frag_blocks`: fragments g * 2 to (g + 1) * 2 - 1 form group g; block b belongs to owner b // 6. Among the 6 entries of one group no owner is named more than 3 times, and group g names owner (g + s) mod 4 exactly 3 times, for a shift s common to all groups. The first and the last block of every owner are named. `frag_signs`: each sign is +1 or -1.
All inputs are finite; a program needn't handle non-finite values.
Results may differ from a plain program's by a relative error of at most 0.0001.
Values sent between devices are 32-bit elements; how exact they have to be, the bound alone decides.
A program may use at most 192 MiB of HBM per device.

v0:
```python
import jax
import jax.numpy as jnp
from jax import lax
from jax.sharding import PartitionSpec as P

FB = 3
ORBS = 128
ITERS = 2
CAP = 3


SPACING = 0.5
FILTER_CENTER = 18.0
FILTER_HALF = 16.0
DENSITY_FLOOR = 0.25
EXCHANGE_COEF = 0.9847450218426965
NORM_EPS = 1e-06


def laplacian(values):
    side_cells = values.shape[-2]
    plane_cells = values.shape[-1]
    leading = [(0, 0)] * (values.ndim - 2)
    padded_x = jnp.pad(values, leading + [(2, 2), (0, 0)])
    nearest = padded_x[..., 1 : side_cells + 1, :] + padded_x[..., 3 : side_cells + 3, :]
    distant = padded_x[..., 0:side_cells, :] + padded_x[..., 4 : side_cells + 4, :]
    padded_y = jnp.pad(values, leading + [(0, 0), (2 * side_cells, 2 * side_cells)])
    nearest = (
        nearest
        + padded_y[..., side_cells : side_cells + plane_cells]
        + padded_y[..., 3 * side_cells : 3 * side_cells + plane_cells]
    )
    distant = (
        distant
        + padded_y[..., 0:plane_cells]
        + padded_y[..., 4 * side_cells : 4 * side_cells + plane_cells]
    )
    padded_z = jnp.pad(values, leading + [(0, 0), (2, 2)])
    column = jnp.arange(plane_cells, dtype=jnp.int32) % side_cells
    nearest = nearest + jnp.where(column >= 1, padded_z[..., 1 : 1 + plane_cells], 0.0)
    nearest = nearest + jnp.where(column <= side_cells - 2, padded_z[..., 3 : 3 + plane_cells], 0.0)
    distant = distant + jnp.where(column >= 2, padded_z[..., 0:plane_cells], 0.0)
    distant = distant + jnp.where(column <= side_cells - 3, padded_z[..., 4 : 4 + plane_cells], 0.0)
    return (16.0 * nearest - distant - 90.0 * values) / 12.0


def hamiltonian(values, local_pot):
    return -0.5 / (SPACING * SPACING) * laplacian(values) + local_pot * values


def chebyshev(values, local_pot):
    previous = values
    current = (hamiltonian(values, local_pot) - FILTER_CENTER * values) / FILTER_HALF
    for degree in range(3):
        further = (
            2.0 * (hamiltonian(current, local_pot) - FILTER_CENTER * current) / FILTER_HALF
            - previous
        )
        previous, current = (current, further)
    magnitude = jnp.sqrt(jnp.mean(current * current, axis=(-2, -1), keepdims=True) + NORM_EPS)
    return current / magnitude


def owner_tables(frag_blocks, block_count, groups):
    entries = frag_blocks.reshape(groups, -1)
    owners = entries // block_count
    count = entries.shape[1]
    positions = jnp.arange(count, dtype=jnp.int32)
    earlier = positions[:, None] > positions[None, :]
    same_owner = owners[:, :, None] == owners[:, None, :]
    ranks = jnp.sum(jnp.where(same_owner & earlier[None, :, :], 1, 0), axis=2).astype(jnp.int32)
    return (entries, owners, ranks)


def assemble(sectioned):
    return lax.all_gather(sectioned, "orb", axis=2, tiled=True)


def reduce_density(partial_value):
    return lax.psum_scatter(partial_value, "orb", scatter_dimension=2, tiled=True)


def filter_group(orbital_group, sectioned, side_cells, plane_cells):
    frag_pot = assemble(sectioned)
    count = orbital_group.shape[0]
    result = chebyshev(orbital_group, frag_pot.reshape(count, 1, side_cells, plane_cells))
    partial_value = jnp.sum(result * result, axis=1).reshape(count, FB, -1)
    return (result, reduce_density(partial_value))


def shards(orbitals, potential, ion_potential, core_density, frag_blocks, frag_signs):
    groups = lax.axis_size("frag")
    me_index = lax.axis_index("frag")
    side_cells = orbitals.shape[2]
    plane_cells = orbitals.shape[3]
    frag_count = orbitals.shape[0]
    block_count = potential.shape[0]
    piece_cells = potential.shape[1]
    capacity = CAP
    entries, owners, ranks = owner_tables(frag_blocks, block_count, groups)
    count = entries.shape[1]
    slot_range = jnp.arange(capacity, dtype=jnp.int32)
    send_match = (owners[:, None, :] == me_index) & (ranks[:, None, :] == slot_range[None, :, None])
    send_valid = jnp.any(send_match, axis=2).reshape(-1)
    send_block = jnp.sum(
        jnp.where(send_match, entries[:, None, :] - me_index * block_count, 0), axis=2
    ).reshape(-1)
    send_mask = send_valid.astype(jnp.float32)[:, None]
    my_owners = lax.dynamic_index_in_dim(owners, me_index, 0, keepdims=False)
    my_ranks = lax.dynamic_index_in_dim(ranks, me_index, 0, keepdims=False)
    my_slot = my_owners * capacity + my_ranks
    owner_range = jnp.arange(groups, dtype=jnp.int32)
    back_match = (my_owners[None, None, :] == owner_range[:, None, None]) & (
        my_ranks[None, None, :] == slot_range[None, :, None]
    )
    back_mask = jnp.any(back_match, axis=2).reshape(-1).astype(jnp.float32)[:, None]
    entry_range = jnp.arange(count, dtype=jnp.int32)
    back_entry = jnp.sum(jnp.where(back_match, entry_range[None, None, :], 0), axis=2).reshape(-1)
    my_signs = jnp.repeat(
        lax.dynamic_slice_in_dim(frag_signs, me_index * frag_count, frag_count), FB
    ).astype(jnp.float32)
    block_range = jnp.arange(block_count, dtype=jnp.int32)
    selector = ((send_block[None, :] == block_range[:, None]) & send_valid[None, :]).astype(
        jnp.float32
    )
    current_pot = potential
    orbital_set = orbitals
    for iteration in range(ITERS):
        outgoing = (jnp.take(current_pot, send_block, axis=0) * send_mask).reshape(
            groups, capacity, piece_cells
        )
        incoming = lax.all_to_all(outgoing, "frag", split_axis=0, concat_axis=0, tiled=True)
        sectioned = jnp.take(
            incoming.reshape(groups * capacity, piece_cells), my_slot, axis=0
        ).reshape(frag_count, FB, piece_cells)
        orbital_set, summed = filter_group(orbital_set, sectioned, side_cells, plane_cells)
        signed = (summed / ORBS).reshape(count, piece_cells) * my_signs[:, None]
        returning = (jnp.take(signed, back_entry, axis=0) * back_mask).reshape(
            groups, capacity, piece_cells
        )
        arrived = lax.all_to_all(returning, "frag", split_axis=0, concat_axis=0, tiled=True)
        collected = jnp.dot(
            selector,
            arrived.reshape(groups * capacity, piece_cells),
            precision=lax.Precision.HIGHEST,
            preferred_element_type=jnp.float32,
        )
        total = core_density + collected
        current_pot = ion_potential - EXCHANGE_COEF * jnp.cbrt(jnp.maximum(total, DENSITY_FLOOR))
    return (orbital_set, current_pot)


def solution(mesh):
    in_specs = (
        P("frag", "orb", None, None),
        P("frag", "orb"),
        P("frag", "orb"),
        P("frag", "orb"),
        P(),
        P(),
    )
    out_specs = (P("frag", "orb", None, None), P("frag", "orb"))
    return jax.shard_map(shards, mesh=mesh, in_specs=in_specs, out_specs=out_specs, check_vma=False)
```

profile of v0, /device:TPU:0, one launch (start us, length us, event | category | flops | bytes accessed | tf_op | source)
XLA Modules:
  0.0 1422.3 jit_solution(12860398454618629138)
XLA Ops:
  17.6 5.6 all-to-all-done
  24.1 17.8 %all_gather.6 = f32[2,3,36864]{2,1,0:T(4,128)S(1)} all-gather(f32[2,3,4608]{2,1,0:T(4,128)S(1)} %reshape.238), channel_id=1, replica_groups=mesh['frag'=4,'orb'=8] {'orb'}, dimensions={2}, use_global_device_ids=true | all-gather | bytes 995328 | tf_op jit(solution)/shard_map/all_gather | solution.py:76
  42.6 95.4 %broadcast_multiply_fusion.1 = (f32[2,16,48,2304]{3,2,1,0:T(8,128)}, f32[2,16,48,2304]{3,2,1,0:T(8,128)}) fusion(f32[2,16,48,2304]{3,2,1,0:T(8,128)} %param.10, f32[2,48,2304]{2,1,0:T(8,128)S(1)} %mul.251, pred[2304]{0:T(1024)(128)(4,1)S(1)} %get-tuple-element.27, pred[2304]{0:T(1024)(128)(4,1)S(1)} %get-tuple-element.28, ...), kind=kLoop, calls=%fused_computation.245 | loop fusion | flops 84934656 | bytes 43361280 | tf_op jit(solution)/shard_map/div | solution.py:53
  138.0 94.8 %fusion.25 = f32[2,16,48,2304]{3,2,1,0:T(8,128)} fusion(f32[2,16,48,2304]{3,2,1,0:T(8,128)} %param.10, f32[2,16,48,2304]{3,2,1,0:T(8,128)} %get-tuple-element.14, f32[2,16,48,2304]{3,2,1,0:T(8,128)} %get-tuple-element.15, f32[2,48,2304]{2,1,0:T(8,128)S(1)} %broadcast_multiply_fusion.3, pred[2304]{0:T(1024)(128)(4,1)S(1)} %get-tuple-element.27, ...), kind=kLoop, calls=%fused_computation.95 | loop fusion | flops 88473600 | bytes 57517056 | tf_op jit(solution)/shard_map/sub | solution.py:56
  232.8 95.9 %fusion.41 = f32[2,16,48,2304]{3,2,1,0:T(8,128)} fusion(f32[2,16,48,2304]{3,2,1,0:T(8,128)} %fusion.25, f32[2,16,48,2304]{3,2,1,0:T(8,128)} %get-tuple-element.15, f32[2,48,2304]{2,1,0:T(8,128)S(1)} %mul.251, pred[2304]{0:T(1024)(128)(4,1)S(1)} %get-tuple-element.27, pred[2304]{0:T(1024)(128)(4,1)S(1)} %get-tuple-element.28, ...), kind=kLoop, calls=%fused_computation.111 | loop fusion | flops 92012544 | bytes 43361280 | tf_op jit(solution)/shard_map/sub | solution.py:56
  328.7 97.0 %multiply_reduce_fusion.3 = (f32[2,16]{1,0:T(2,128)S(1)}, f32[2,16,48,2304]{3,2,1,0:T(8,128)}) fusion(f32[2,16,48,2304]{3,2,1,0:T(8,128)} %fusion.25, f32[2,16,48,2304]{3,2,1,0:T(8,128)} %fusion.41, f32[2,48,2304]{2,1,0:T(8,128)S(1)} %mul.251, pred[2304]{0:T(1024)(128)(4,1)S(1)} %get-tuple-element.27, pred[2304]{0:T(1024)(128)(4,1)S(1)} %get-tuple-element.28, ...), kind=kLoop, calls=%fused_computation.227 | loop fusion | flops 95551456 | bytes 43361408 | tf_op jit(solution)/shard_map/reduce_sum | solution.py:60
  425.8 12.4 multiply_reduce_fusion.2
  438.7 32.8 %copy.35 = f32[2,3,36864]{1,0,2:T(2,128)} copy(f32[2,3,36864]{2,1,0:T(4,128)S(1)} %reshape.239) | data formatting | bytes 1769472
  471.4 35.1 %reshape.318 = f32[36864,6]{1,0:T(8,128)} reshape(f32[36864,2,3]{2,1,0:T(2,128)} %bitcast.9) | data formatting | bytes 1769472
  507.8 186.1 %reduce-scatter.7.cloned.1.call-done = f32[4608,6]{1,0:T(8,128)} async-done(((f32[36864,6]{1,0:T(8,128)}), f32[4608,6]{1,0:T(8,128)}) %reduce-scatter.7.cloned.1.call-update) | async-done | bytes 110608
  694.0 5.8 reshape.319
  706.3 9.6 all_to_all.20
  717.3 8.5 all_to_all.21
  726.6 17.0 %all_gather.7 = f32[2,3,36864]{2,1,0:T(4,128)S(1)} all-gather(f32[2,3,4608]{2,1,0:T(4,128)S(1)} %reshape.246), channel_id=1, replica_groups=mesh['frag'=4,'orb'=8] {'orb'}, dimensions={2}, use_global_device_ids=true | all-gather | bytes 995328 | tf_op jit(solution)/shard_map/all_gather | solution.py:76
  744.4 94.5 %broadcast_multiply_fusion = (f32[2,16,48,2304]{3,2,1,0:T(8,128)}, f32[2,16,48,2304]{3,2,1,0:T(8,128)}) fusion(f32[2,16,48,2304]{3,2,1,0:T(8,128)} %get-tuple-element.11, f32[2,48,2304]{2,1,0:T(8,128)S(1)} %mul.287, pred[2304]{0:T(1024)(128)(4,1)S(1)} %get-tuple-element.27, pred[2304]{0:T(1024)(128)(4,1)S(1)} %get-tuple-element.28, ...), kind=kLoop, calls=%fused_computation.244 | loop fusion | flops 84934656 | bytes 43361280 | tf_op jit(solution)/shard_map/div | solution.py:53
  838.9 94.2 %fusion.87 = f32[2,16,48,2304]{3,2,1,0:T(8,128)} fusion(f32[2,16,48,2304]{3,2,1,0:T(8,128)} %get-tuple-element.11, f32[2,16,48,2304]{3,2,1,0:T(8,128)} %get-tuple-element.8, f32[2,16,48,2304]{3,2,1,0:T(8,128)} %get-tuple-element.9, f32[2,48,2304]{2,1,0:T(8,128)S(1)} %broadcast_multiply_fusion.2, pred[2304]{0:T(1024)(128)(4,1)S(1)} %get-tuple-element.27, ...), kind=kLoop, calls=%fused_computation.157 | loop fusion | flops 88473600 | bytes 57517056 | tf_op jit(solution)/shard_map/sub | solution.py:56
  933.1 96.2 %fusion.103 = f32[2,16,48,2304]{3,2,1,0:T(8,128)} fusion(f32[2,16,48,2304]{3,2,1,0:T(8,128)} %fusion.87, f32[2,48,2304]{2,1,0:T(8,128)S(1)} %mul.287, f32[2,16,48,2304]{3,2,1,0:T(8,128)} %get-tuple-element.9, pred[2304]{0:T(1024)(128)(4,1)S(1)} %get-tuple-element.27, pred[2304]{0:T(1024)(128)(4,1)S(1)} %get-tuple-element.28, ...), kind=kLoop, calls=%fused_computation.173 | loop fusion | flops 92012544 | bytes 43361280 | tf_op jit(solution)/shard_map/sub | solution.py:56
  1029.4 96.3 %multiply_reduce_fusion.1 = (f32[2,16]{1,0:T(2,128)S(1)}, f32[2,16,48,2304]{3,2,1,0:T(8,128)}) fusion(f32[2,16,48,2304]{3,2,1,0:T(8,128)} %fusion.87, f32[2,16,48,2304]{3,2,1,0:T(8,128)} %fusion.103, f32[2,48,2304]{2,1,0:T(8,128)S(1)} %mul.287, pred[2304]{0:T(1024)(128)(4,1)S(1)} %get-tuple-element.27, pred[2304]{0:T(1024)(128)(4,1)S(1)} %get-tuple-element.28, ...), kind=kLoop, calls=%fused_computation.211 | loop fusion | flops 95551456 | bytes 43361408 | tf_op jit(solution)/shard_map/reduce_sum | solution.py:60
  1125.7 12.4 multiply_reduce_fusion
  1138.6 32.8 %copy.37 = f32[2,3,36864]{1,0,2:T(2,128)} copy(f32[2,3,36864]{2,1,0:T(4,128)S(1)} %reshape.247) | data formatting | bytes 1769472
  1171.4 35.1 %reshape.320 = f32[36864,6]{1,0:T(8,128)} reshape(f32[36864,2,3]{2,1,0:T(2,128)} %bitcast.10) | data formatting | bytes 1769472
  1206.5 185.6 %reduce-scatter.9.cloned.1.call-done = f32[4608,6]{1,0:T(8,128)} async-done(((f32[36864,6]{1,0:T(8,128)}), f32[4608,6]{1,0:T(8,128)}) %reduce-scatter.9.cloned.1.call-update) | async-done | bytes 110608
  1392.1 5.8 reshape.321
  1404.5 9.6 all_to_all.22
  (96 shorter events, 31.2 us)
Async XLA Ops:
  7.2 3.7 copy-start
  12.4 10.8 all-to-all-start
  17.6 676.4 %reduce-scatter.7.cloned.1.call-start = ((), (), s32[]{:S(2)}) async-start(), calls=%async_computation.6 | async-start | bytes 21233664
  506.6 0.7 copy-start.4
  506.6 209.5 %copy-start.2 = (f32[6,4608]{1,0:T(8,128)S(1)}, f32[6,4608]{1,0:T(8,128)}, u32[]{:S(2)}) copy-start(f32[6,4608]{1,0:T(8,128)} %param.12) | copy-start | bytes 331780
  506.6 209.5 %copy-start.3 = (f32[6,4608]{1,0:T(8,128)S(1)}, f32[6,4608]{1,0:T(8,128)}, u32[]{:S(2)}) copy-start(f32[6,4608]{1,0:T(8,128)} %param.13) | copy-start | bytes 331780
  506.6 885.5 %reduce-scatter.9.cloned.1.call-start = ((), (), s32[]{:S(2)}) async-start(), calls=%async_computation.7 | async-start | bytes 21233664
  1206.5 208.7 %copy-start.1 = (f32[6,4608]{1,0:T(8,128)S(1)}, f32[6,4608]{1,0:T(8,128)}, u32[]{:S(2)}) copy-start(f32[6,4608]{1,0:T(8,128)} %param.11) | copy-start | bytes 331780
Sparse Core Ops, SparseCore 0:
  506.7 187.1 reduce-scatter.6
  1206.6 185.4 reduce-scatter.8
where the time goes:
time: 1430 us; the launch traced here: 1420 us
  other arithmetic  793 us (55%)
  waiting for transfers between devices  377 us (26%)
  local copies, waits for them, and re-layouts  169 us (12%)
  blocking collectives  62.6 us (4%)
  between operations  14.6 us (1%)
    sub x4, other arithmetic, chebyshev(): 2.0 * (hamiltonian(current, local_pot) - FILTER_CENTER * current)  381 us
    unnamed x4, waiting for transfers between devices  372 us
    reduce_sum x2, other arithmetic, chebyshev(): jnp.mean(current * current, axis=(-2, -1), keepdims=True) + NORM_EPS  193 us
    div x2, other arithmetic, chebyshev(): (hamiltonian(values, local_pot) - FILTER_CENTER * values) / FILTER_HALF  190 us
    unnamed x18, local copies, waits for them, and re-layouts  159 us
    all_gather x2, blocking collectives, assemble(): return lax.all_gather(sectioned, 'orb', axis=2, tiled=True)  34.8 us
  transfers between devices with their start and end apart: 3, of which 3 were waited for; matrix products, arithmetic and copies ran while one was open for 0% of the time, Pallas kernels for 0%

commit v1 on v0

v1 whole, which is shorter than its diff:
```python
import functools

import jax
import jax.numpy as jnp
import numpy as np
from jax import lax
from jax.experimental import pallas as pl
from jax.experimental.pallas import tpu as pltpu
from jax.sharding import PartitionSpec as P

FB = 3
ORBS = 128
ITERS = 2
CAP = 3

DENSITY_FLOOR = 0.25
EXCHANGE_COEF = 0.9847450218426965
NORM_EPS = 1e-06

LANE = 128
NB = 256


def band_weights(side):
    period = side // np.gcd(NB, side)
    mats = []
    for phase in range(int(period)):
        out = NB * phase + np.arange(NB)[None, :]
        inp = NB * phase - LANE + np.arange(NB + 2 * LANE)[:, None]
        diff = inp - out
        same = (inp // side) == (out // side)
        near = (same & (np.abs(diff) == 1)) | (np.abs(diff) == side)
        far = (same & (np.abs(diff) == 2)) | (np.abs(diff) == 2 * side)
        mat = np.where(near, -16.0, 0.0) + np.where(far, 1.0, 0.0)
        mat = mat.reshape(-1, 1, LANE, NB)
        mats.append(np.concatenate([mat, mat], axis=1).reshape(-1, NB))
    return jnp.asarray(np.stack(mats), dtype=jnp.bfloat16)


def filter_kernel(first, frag, orbs, side, plane, *refs):
    orb_ref, pot_ref, band_ref = refs[:3]
    out_ref, dens_ref, ybuf, zbuf, hly, hlz, wbuf, sems = refs[-8:]
    blocks = plane // NB
    tiles = plane // LANE
    period = band_ref.shape[0]
    xc = 16 // orbs
    rows_chunk = orbs * side // 3
    x_chunk = rows_chunk // 16
    inv48 = 1.0 / 48.0

    if first:
        copies = [
            pltpu.make_async_copy(
                orb_ref.at[frag, o], ybuf.at[pl.ds(2, side), o, :], sems.at[o]
            )
            for o in range(orbs)
        ]
    else:
        copies = [pltpu.make_async_copy(orb_ref, ybuf.at[pl.ds(2, side)], sems.at[0])]
    for copy in copies:
        copy.start()
    wbuf[...] = (pot_ref[...] - 3.0) * 0.125
    for buf in (ybuf, zbuf):
        buf[pl.ds(0, 2)] = jnp.zeros((2, orbs, plane), jnp.float32)
        buf[pl.ds(side + 2, 2)] = jnp.zeros((2, orbs, plane), jnp.float32)
    rows = hly.shape[0]
    for buf in (hly, hlz):
        buf[:, pl.ds(0, NB)] = jnp.zeros((rows, NB), jnp.bfloat16)
        buf[:, pl.ds(NB * (tiles + 1), NB)] = jnp.zeros((rows, NB), jnp.bfloat16)
    for copy in copies:
        copy.wait()

    def split(dst, row, lane, new):
        high = new.astype(jnp.bfloat16)
        low = (new - high.astype(jnp.float32)).astype(jnp.bfloat16)
        for half in range(NB // LANE):
            part = slice(half * LANE, (half + 1) * LANE)
            at = pl.multiple_of(2 * lane + NB * (half + 1), NB)
            dst[pl.ds(row, 16), pl.ds(at, LANE)] = high[:, part]
            dst[pl.ds(row, 16), pl.ds(at + LANE, LANE)] = low[:, part]

    def split_block(i, carry):
        x = i * xc
        for b in range(blocks):
            value = ybuf[pl.ds(x + 2, xc), :, pl.ds(b * NB, NB)].reshape(16, NB)
            split(hly, pl.multiple_of(i * 16, 16), b * NB, value)
        return carry

    lax.fori_loop(0, side // xc, split_block, 0)

    def step(cur, dst, hl_cur, hl_next, start, last):
        def block(b, carry):
            lane = pl.multiple_of(b * NB, NB)
            weights = band_ref[lax.rem(b, period)]

            def product(c):
                return jnp.dot(
                    hl_cur[pl.ds(c * rows_chunk, rows_chunk), pl.ds(2 * lane, 4 * NB)],
                    weights,
                    preferred_element_type=jnp.float32,
                )

            def update(c, prod, acc):
                for j in range(x_chunk):
                    i = c * x_chunk + j
                    x = i * xc

                    def plane_at(buf, offset):
                        return buf[pl.ds(x + 2 + offset, xc), :, pl.ds(lane, NB)].reshape(16, NB)

                    near = plane_at(cur, -1) + plane_at(cur, 1)
                    far = plane_at(cur, -2) + plane_at(cur, 2)
                    total = prod[j * 16 : (j + 1) * 16] + (far - 16.0 * near)
                    w = wbuf[pl.ds(x, xc), pl.ds(lane, NB)]
                    w = jnp.broadcast_to(w[:, None, :], (xc, orbs, NB)).reshape(16, NB)
                    new = total * inv48 + w * plane_at(cur, 0)
                    if start:
                        new = new * 0.5
                    else:
                        new = new - plane_at(dst, 0)
                    dst[pl.ds(x + 2, xc), :, pl.ds(lane, NB)] = new.reshape(xc, orbs, NB)
                    if last:
                        acc = acc + new * new
                    else:
                        split(hl_next, i * 16, lane, new)
                return acc

            acc = carry
            count = rows // rows_chunk
            prods = [product(0)]
            for c in range(count):
                if c + 1 < count:
                    prods.append(product(c + 1))
                acc = update(c, prods[c], acc)
            return acc

        return lax.fori_loop(0, blocks, block, jnp.zeros((16, NB), jnp.float32))

    step(ybuf, zbuf, hly, hlz, True, False)
    step(zbuf, ybuf, hlz, hly, False, False)
    step(ybuf, zbuf, hly, hlz, False, False)
    acc = step(zbuf, ybuf, hlz, hly, False, True)
    square = jnp.sum(acc, axis=1, keepdims=True).reshape(xc, orbs, 1)
    square = jnp.sum(square, axis=0)
    scale = 1.0 / jnp.sqrt(square * (1.0 / (side * plane)) + NORM_EPS)
    scale = jnp.broadcast_to(scale, (orbs, NB))

    def finish(i, carry):
        x = pl.multiple_of(i * 8, 8)
        for b in range(blocks):
            lanes = pl.ds(b * NB, NB)
            value = ybuf[pl.ds(x + 2, 8), :, lanes] * scale[None]
            ybuf[pl.ds(x + 2, 8), :, lanes] = value
            dens_ref[pl.ds(x, 8), lanes] = jnp.sum(value * value, axis=1)
        return carry

    lax.fori_loop(0, side // 8, finish, 0)
    if first:
        outs = [pltpu.make_async_copy(ybuf.at[pl.ds(2, side)], out_ref, sems.at[0])]
    else:
        outs = [
            pltpu.make_async_copy(
                ybuf.at[pl.ds(2, side), o, :], out_ref.at[frag, o], sems.at[o]
            )
            for o in range(orbs)
        ]
    for copy in outs:
        copy.start()
    for copy in outs:
        copy.wait()


def filter_call(first, frag, shape, source, pot, band, previous):
    count, orbs, side, plane = shape
    rows = orbs * side
    body = functools.partial(filter_kernel, first, frag, orbs, side, plane)
    vmem = pl.BlockSpec(memory_space=pltpu.VMEM)
    hbm = pl.BlockSpec(memory_space=pl.ANY)
    in_specs = [hbm, vmem, vmem]
    operands = [source, pot, band]
    aliases = {}
    if first:
        out = jax.ShapeDtypeStruct((side, orbs, plane), jnp.float32)
    else:
        out = jax.ShapeDtypeStruct(shape, jnp.float32)
        if previous is not None:
            in_specs.append(hbm)
            operands.append(previous)
            aliases = {3: 0}
    wide = 2 * plane + 2 * NB
    return pl.pallas_call(
        body,
        out_shape=(out, jax.ShapeDtypeStruct((side, plane), jnp.float32)),
        in_specs=in_specs,
        out_specs=(hbm, vmem),
        input_output_aliases=aliases,
        scratch_shapes=[
            pltpu.VMEM((side + 4, orbs, plane), jnp.float32),
            pltpu.VMEM((side + 4, orbs, plane), jnp.float32),
            pltpu.VMEM((rows, wide), jnp.bfloat16),
            pltpu.VMEM((rows, wide), jnp.bfloat16),
            pltpu.VMEM((side, plane), jnp.float32),
            pltpu.SemaphoreType.DMA((orbs,)),
        ],
        compiler_params=pltpu.CompilerParams(vmem_limit_bytes=48 * 1024 * 1024),
        cost_estimate=pl.CostEstimate(
            flops=4 * 2 * rows * plane * 1024,
            bytes_accessed=8 * rows * plane,
            transcendentals=0,
        ),
        name="filter_fragment",
    )(*operands)


def owner_tables(frag_blocks, block_count, groups):
    entries = frag_blocks.reshape(groups, -1)
    owners = entries // block_count
    count = entries.shape[1]
    positions = jnp.arange(count, dtype=jnp.int32)
    earlier = positions[:, None] > positions[None, :]
    same_owner = owners[:, :, None] == owners[:, None, :]
    ranks = jnp.sum(jnp.where(same_owner & earlier[None, :, :], 1, 0), axis=2).astype(jnp.int32)
    return (entries, owners, ranks)


def shards(orbitals, potential, ion_potential, core_density, frag_blocks, frag_signs):
    groups = lax.axis_size("frag")
    me_index = lax.axis_index("frag")
    side = orbitals.shape[2]
    plane = orbitals.shape[3]
    frag_count = orbitals.shape[0]
    block_count = potential.shape[0]
    piece_cells = potential.shape[1]
    capacity = CAP
    band = band_weights(side)
    entries, owners, ranks = owner_tables(frag_blocks, block_count, groups)
    count = entries.shape[1]
    slot_range = jnp.arange(capacity, dtype=jnp.int32)
    send_match = (owners[:, None, :] == me_index) & (ranks[:, None, :] == slot_range[None, :, None])
    send_valid = jnp.any(send_match, axis=2).reshape(-1)
    send_block = jnp.sum(
        jnp.where(send_match, entries[:, None, :] - me_index * block_count, 0), axis=2
    ).reshape(-1)
    send_mask = send_valid.astype(jnp.float32)[:, None]
    my_owners = lax.dynamic_index_in_dim(owners, me_index, 0, keepdims=False)
    my_ranks = lax.dynamic_index_in_dim(ranks, me_index, 0, keepdims=False)
    my_slot = my_owners * capacity + my_ranks
    owner_range = jnp.arange(groups, dtype=jnp.int32)
    back_match = (my_owners[None, None, :] == owner_range[:, None, None]) & (
        my_ranks[None, None, :] == slot_range[None, :, None]
    )
    back_mask = jnp.any(back_match, axis=2).reshape(-1).astype(jnp.float32)[:, None]
    entry_range = jnp.arange(count, dtype=jnp.int32)
    back_entry = jnp.sum(jnp.where(back_match, entry_range[None, None, :], 0), axis=2).reshape(-1)
    my_signs = jnp.repeat(
        lax.dynamic_slice_in_dim(frag_signs, me_index * frag_count, frag_count), FB
    ).astype(jnp.float32)
    block_range = jnp.arange(block_count, dtype=jnp.int32)
    selector = ((send_block[None, :] == block_range[:, None]) & send_valid[None, :]).astype(
        jnp.float32
    )
    current_pot = potential
    middle = None
    filtered = None
    for iteration in range(ITERS):
        outgoing = (jnp.take(current_pot, send_block, axis=0) * send_mask).reshape(
            groups, capacity, piece_cells
        )
        incoming = lax.all_to_all(outgoing, "frag", split_axis=0, concat_axis=0, tiled=True)
        sectioned = jnp.take(
            incoming.reshape(groups * capacity, piece_cells), my_slot, axis=0
        ).reshape(frag_count, FB, piece_cells)
        pieces = []
        next_middle = []
        for frag in range(frag_count):
            pot = lax.all_gather(sectioned[frag], "orb", axis=1, tiled=True).reshape(side, plane)
            if iteration == 0:
                result, dens = filter_call(True, frag, orbitals.shape, orbitals, pot, band, None)
                next_middle.append(result)
            else:
                filtered, dens = filter_call(
                    False, frag, orbitals.shape, middle[frag], pot, band, filtered
                )
            pieces.append(
                lax.psum_scatter(dens.reshape(FB, -1), "orb", scatter_dimension=1, tiled=True)
            )
        middle = next_middle
        summed = jnp.stack(pieces)
        signed = (summed / ORBS).reshape(count, piece_cells) * my_signs[:, None]
        returning = (jnp.take(signed, back_entry, axis=0) * back_mask).reshape(
            groups, capacity, piece_cells
        )
        arrived = lax.all_to_all(returning, "frag", split_axis=0, concat_axis=0, tiled=True)
        collected = jnp.dot(
            selector,
            arrived.reshape(groups * capacity, piece_cells),
            precision=lax.Precision.HIGHEST,
            preferred_element_type=jnp.float32,
        )
        total = core_density + collected
        current_pot = ion_potential - EXCHANGE_COEF * jnp.cbrt(jnp.maximum(total, DENSITY_FLOOR))
    return (filtered, current_pot)


def solution(mesh):
    in_specs = (
        P("frag", "orb", None, None),
        P("frag", "orb"),
        P("frag", "orb"),
        P("frag", "orb"),
        P(),
        P(),
    )
    out_specs = (P("frag", "orb", None, None), P("frag", "orb"))
    return jax.shard_map(shards, mesh=mesh, in_specs=in_specs, out_specs=out_specs, check_vma=False)
```

time: 1430 us -> 978 us (0.68)
  other arithmetic: 793 us -> 3.22 us
  waiting for transfers between devices: 377 us -> 654 us
  Pallas kernels: 0 us -> 150 us
  local copies, waits for them, and re-layouts: 169 us -> 61.3 us
  blocking collectives: 62.6 us -> 88.4 us
    sub x4 -> x0, other arithmetic: 381 us -> none  [chebyshev(): 2.0 * (hamiltonian(current, local_pot) - FILTER_CENTER * current)]
    unnamed x4 -> x8, waiting for transfers between devices: 372 us -> 648 us
    reduce_sum x4 -> x0, other arithmetic: 218 us -> none  [the longest x2 193 us: chebyshev(): jnp.mean(current * current, axis=(-2, -1), keepdims=True) + NORM_EPS]
    div x4 -> x0, other arithmetic: 190 us -> none  [the longest x2 190 us: chebyshev(): (hamiltonian(values, local_pot) - FILTER_CENTER * values) / FILTER_HALF]
    pallas_call x0 -> x4, Pallas kernels: none -> 150 us  [filter_call(): pl.pallas_call(body, out_shape=(out, jax.ShapeDtypeStruct((side, plane),...]
    unnamed x18 -> x26, local copies, waits for them, and re-layouts: 159 us -> 51.9 us
    all_gather x2 -> x4, blocking collectives: 34.8 us -> 60.6 us  [shards(): lax.all_gather(sectioned[frag], 'orb', axis=1, tiled=True)]
  transfers between devices with their start and end apart: 3 -> 5, of which waited for: 3 -> 5; matrix products, arithmetic and copies ran while one was open for 0% -> 3% of each run, Pallas kernels for 0% -> 8%
where the time goes in v1:
time: 978 us
  waiting for transfers between devices  654 us (67%)
  Pallas kernels  150 us (15%)
  blocking collectives  88.4 us (9%)
  local copies, waits for them, and re-layouts  61.3 us (6%)
  between operations  14.1 us (1%)
    unnamed x8, waiting for transfers between devices  648 us
    pallas_call x4, Pallas kernels, filter_call(): pl.pallas_call(body, out_shape=(out, jax.ShapeDtypeStruct((side, plane),...  150 us
    all_gather x4, blocking collectives, shards(): lax.all_gather(sectioned[frag], 'orb', axis=1, tiled=True)  60.6 us
    unnamed x26, local copies, waits for them, and re-layouts  51.9 us
  transfers between devices with their start and end apart: 5, of which 5 were waited for; matrix products, arithmetic and copies ran while one was open for 3% of the time, Pallas kernels for 8%

profile of v1, /device:TPU:0, one launch (start us, length us, event | category | flops | bytes accessed | tf_op | source)
XLA Modules:
  0.0 977.6 jit_solution(13056129320948862281)
XLA Ops:
  12.4 5.2 all-to-all-start
  17.6 5.6 all-to-all-done
  24.1 15.2 %all_gather.13 = f32[3,36864]{1,0:T(4,128)S(1)} all-gather(f32[3,4608]{1,0:T(4,128)S(1)} %get-tuple-element.27), channel_id=1, replica_groups=mesh['frag'=4,'orb'=8] {'orb'}, dimensions={1}, use_global_device_ids=true | all-gather | bytes 497664 | tf_op jit(solution)/shard_map/all_gather | solution.py:276
  39.6 15.0 %all_gather.12 = f32[3,36864]{1,0:T(4,128)S(1)} all-gather(f32[3,4608]{1,0:T(4,128)S(1)} %get-tuple-element.28), channel_id=1, replica_groups=mesh['frag'=4,'orb'=8] {'orb'}, dimensions={1}, use_global_device_ids=true | all-gather | bytes 497664 | tf_op jit(solution)/shard_map/all_gather | solution.py:276
  56.4 37.4 %filter_fragment.5 = (f32[48,16,2304]{2,1,0:T(8,128)}, f32[48,2304]{1,0:T(8,128)S(1)}) custom-call(f32[2,16,48,2304]{3,2,1,0:T(8,128)} %refs_0_.3, f32[48,2304]{1,0:T(8,128)S(1)} %reshape.241.refs_1_, bf16[3,1024,256]{2,1,0:T(8,128)(2,1)S(1)} %copy-done.2), custom_call_target="tpu_custom_call" | custom-call | flops 14495514624 | bytes 14155776 | tf_op jit(solution)/shard_map/filter_fragment/pallas_call | solution.py:191
  94.0 9.9 %copy.37 = f32[3,36864]{0,1:T(8,128)} copy(f32[3,36864]{1,0:T(4,128)S(1)} %reshape.242) | data formatting | bytes 884736
  105.3 37.3 %filter_fragment.4 = (f32[48,16,2304]{2,1,0:T(8,128)}, f32[48,2304]{1,0:T(8,128)S(1)}) custom-call(f32[2,16,48,2304]{3,2,1,0:T(8,128)} %refs_0_.3, f32[48,2304]{1,0:T(8,128)S(1)} %reshape.240.refs_1_, bf16[3,1024,256]{2,1,0:T(8,128)(2,1)S(1)} %copy-done.3), custom_call_target="tpu_custom_call" | custom-call | flops 14495514624 | bytes 14155776 | tf_op jit(solution)/shard_map/filter_fragment/pallas_call | solution.py:191
  142.9 9.8 %copy.39 = f32[3,36864]{0,1:T(8,128)} copy(f32[3,36864]{1,0:T(4,128)S(1)} %reshape.243) | data formatting | bytes 884736
  153.9 138.7 %reduce-scatter.13.cloned.1.call-done = f32[4608,3]{1,0:T(8,128)} async-done(((f32[36864,3]{1,0:T(8,128)}), f32[4608,3]{1,0:T(8,128)}) %reduce-scatter.13.cloned.1.call-update) | async-done | bytes 55312
  292.6 2.4 copy.38
  294.9 186.3 %reduce-scatter.15.cloned.1.call-done = f32[4608,3]{1,0:T(8,128)} async-done(((f32[36864,3]{1,0:T(8,128)}), f32[4608,3]{1,0:T(8,128)}) %reduce-scatter.15.cloned.1.call-update) | async-done | bytes 55312
  484.6 9.6 all_to_all.20
  495.6 8.5 all_to_all.21
  504.9 15.0 %all_gather.15 = f32[3,36864]{1,0:T(4,128)S(1)} all-gather(f32[3,4608]{1,0:T(4,128)S(1)} %get-tuple-element.25), channel_id=1, replica_groups=mesh['frag'=4,'orb'=8] {'orb'}, dimensions={1}, use_global_device_ids=true | all-gather | bytes 497664 | tf_op jit(solution)/shard_map/all_gather | solution.py:276
  520.3 15.4 %all_gather.14 = f32[3,36864]{1,0:T(4,128)S(1)} all-gather(f32[3,4608]{1,0:T(4,128)S(1)} %get-tuple-element.26), channel_id=1, replica_groups=mesh['frag'=4,'orb'=8] {'orb'}, dimensions={1}, use_global_device_ids=true | all-gather | bytes 497664 | tf_op jit(solution)/shard_map/all_gather | solution.py:276
  536.0 37.4 %filter_fragment.6 = (f32[2,16,48,2304]{3,2,1,0:T(8,128)}, f32[48,2304]{1,0:T(8,128)S(1)}) custom-call(f32[48,16,2304]{2,1,0:T(8,128)} %get-tuple-element.15.refs_0_, f32[48,2304]{1,0:T(8,128)S(1)} %reshape.250.refs_1_, bf16[3,1024,256]{2,1,0:T(8,128)(2,1)S(1)} %copy-done.3), custom_call_target="tpu_custom_call" | custom-call | flops 14495514624 | bytes 14155776 | tf_op jit(solution)/shard_map/filter_fragment/pallas_call | solution.py:191
  573.6 9.9 %copy.41 = f32[3,36864]{0,1:T(8,128)} copy(f32[3,36864]{1,0:T(4,128)S(1)} %reshape.251) | data formatting | bytes 884736
  583.8 37.8 %filter_fragment.7 = (f32[2,16,48,2304]{3,2,1,0:T(8,128)}, f32[48,2304]{1,0:T(8,128)S(1)}) custom-call(f32[48,16,2304]{2,1,0:T(8,128)} %get-tuple-element.12.refs_0_, f32[48,2304]{1,0:T(8,128)S(1)} %reshape.249.refs_1_, bf16[3,1024,256]{2,1,0:T(8,128)(2,1)S(1)} %copy-done.3, ...), custom_call_target="tpu_custom_call", output_to_operand_aliasing={{0}: (3, {})} | custom-call | flops 14495514624 | bytes 14155776 | tf_op jit(solution)/shard_map/filter_fragment/pallas_call | solution.py:191
  621.9 9.8 %copy.43 = f32[3,36864]{0,1:T(8,128)} copy(f32[3,36864]{1,0:T(4,128)S(1)} %reshape.252) | data formatting | bytes 884736
  631.7 136.6 %reduce-scatter.17.cloned.1.call-done = f32[4608,3]{1,0:T(8,128)} async-done(((f32[36864,3]{1,0:T(8,128)}), f32[4608,3]{1,0:T(8,128)}) %reduce-scatter.17.cloned.1.call-update) | async-done | bytes 55312
  768.3 2.4 copy.42
  770.7 186.2 %reduce-scatter.19.cloned.1.call-done = f32[4608,3]{1,0:T(8,128)} async-done(((f32[36864,3]{1,0:T(8,128)}), f32[4608,3]{1,0:T(8,128)}) %reduce-scatter.19.cloned.1.call-update) | async-done | bytes 55312
  956.9 2.4 copy.44
  960.3 9.6 all_to_all.22
  (104 shorter events, 20.2 us)
Async XLA Ops:
  7.2 3.7 copy-start
  12.4 10.8 %all-to-all-start = ((f32[4,3,4608]{2,1,0:T(4,128)}), f32[4,3,4608]{2,1,0:T(4,128)S(1)}, u32[]{:S(2)}, u32[]{:S(2)}) async-start(f32[4,3,4608]{2,1,0:T(4,128)} %reshape.238), calls=%async_computation | async-start | bytes 589824 | tf_op jit(solution)/shard_map/all_to_all | solution.py:269
  17.6 275.0 %reduce-scatter.13.cloned.1.call-start = ((), (), s32[]{:S(2)}) async-start(), calls=%async_computation.8 | async-start | bytes 21233664
  55.0 1.4 copy-start.2
  103.9 1.4 copy-start.3
  103.9 377.4 %reduce-scatter.15.cloned.1.call-start = ((), (), s32[]{:S(2)}) async-start(), calls=%async_computation.9 | async-start | bytes 21233664
  152.6 0.7 copy-start.8
  152.6 341.7 %copy-start.4 = (f32[6,4608]{1,0:T(8,128)S(1)}, f32[6,4608]{1,0:T(8,128)}, u32[]{:S(2)}) copy-start(f32[6,4608]{1,0:T(8,128)} %param.13) | copy-start | bytes 331780
  152.7 341.7 %copy-start.6 = (f32[6,4608]{1,0:T(8,128)S(1)}, f32[6,4608]{1,0:T(8,128)}, u32[]{:S(2)}) copy-start(f32[6,4608]{1,0:T(8,128)} %param.14) | copy-start | bytes 331780
  152.7 615.7 %reduce-scatter.17.cloned.1.call-start = ((), (), s32[]{:S(2)}) async-start(), calls=%async_computation.10 | async-start | bytes 21233664
  583.5 373.4 %reduce-scatter.19.cloned.1.call-start = ((), (), s32[]{:S(2)}) async-start(), calls=%async_computation.11 | async-start | bytes 21233664
  631.7 339.4 %copy-start.1 = (f32[6,4608]{1,0:T(8,128)S(1)}, f32[6,4608]{1,0:T(8,128)}, u32[]{:S(2)}) copy-start(f32[6,4608]{1,0:T(8,128)} %param.12) | copy-start | bytes 331780
  631.7 338.4 %copy-start.5 = (f32[6,4608]{1,0:T(8,128)S(1)}, f32[6,4608]{1,0:T(8,128)}, u32[]{:S(2)}) copy-start(f32[6,4608]{1,0:T(8,128)} %param.13) | copy-start | bytes 331780
  631.7 338.4 %copy-start.7 = (f32[6,4608]{1,0:T(8,128)S(1)}, f32[6,4608]{1,0:T(8,128)}, u32[]{:S(2)}) copy-start(f32[6,4608]{1,0:T(8,128)} %param.14) | copy-start | bytes 331780
Sparse Core Ops, SparseCore 0:
  104.0 188.4 reduce-scatter.12
  294.9 186.2 reduce-scatter.14
  583.6 184.6 reduce-scatter.16
  770.5 186.3 reduce-scatter.18

commit v2 on v1

--- a/solution.py
+++ b/solution.py
@@ -59,7 +59,13 @@
         copies = [pltpu.make_async_copy(orb_ref, ybuf.at[pl.ds(2, side)], sems.at[0])]
     for copy in copies:
         copy.start()
-    wbuf[...] = (pot_ref[...] - 3.0) * 0.125
+    pieces, _, piece_rows, _ = pot_ref.shape
+    piece_x = piece_rows // FB
+    for d in range(pieces):
+        for slot in range(FB):
+            x = slot * (side // FB) + d * piece_x
+            value = pot_ref[d, frag, slot * piece_x : (slot + 1) * piece_x]
+            wbuf[x : x + piece_x] = (value - 3.0) * 0.125
     for buf in (ybuf, zbuf):
         buf[pl.ds(0, 2)] = jnp.zeros((2, orbs, plane), jnp.float32)
         buf[pl.ds(side + 2, 2)] = jnp.zeros((2, orbs, plane), jnp.float32)
@@ -145,18 +151,29 @@
     scale = 1.0 / jnp.sqrt(square * (1.0 / (side * plane)) + NORM_EPS)
     scale = jnp.broadcast_to(scale, (orbs, NB))
 
-    def finish(i, carry):
-        x = pl.multiple_of(i * 8, 8)
+    def finish(d, carry):
+        starts = [slot * (side // FB) + d * piece_x + 2 for slot in range(FB)]
         for b in range(blocks):
             lanes = pl.ds(b * NB, NB)
-            value = ybuf[pl.ds(x + 2, 8), :, lanes] * scale[None]
-            ybuf[pl.ds(x + 2, 8), :, lanes] = value
-            dens_ref[pl.ds(x, 8), lanes] = jnp.sum(value * value, axis=1)
+            sums = []
+            for start in starts:
+                value = ybuf[pl.ds(start, piece_x), :, lanes] * scale[None]
+                ybuf[pl.ds(start, piece_x), :, lanes] = value
+                sums.append(value * value)
+            dens_ref[d, :, lanes] = jnp.sum(jnp.concatenate(sums, axis=0), axis=1)
+        if first:
+            for start in starts:
+                slab(start).start()
         return carry
 
-    lax.fori_loop(0, side // 8, finish, 0)
+    def slab(start):
+        rows_in = pl.ds(start, piece_x)
+        rows_out = pl.ds(start - 2, piece_x)
+        return pltpu.make_async_copy(ybuf.at[rows_in], out_ref.at[rows_out], sems.at[0])
+
+    lax.fori_loop(0, pieces, finish, 0)
     if first:
-        outs = [pltpu.make_async_copy(ybuf.at[pl.ds(2, side)], out_ref, sems.at[0])]
+        pltpu.make_async_copy(ybuf.at[pl.ds(2, side)], out_ref, sems.at[0]).wait()
     else:
         outs = [
             pltpu.make_async_copy(
@@ -164,10 +181,10 @@
             )
             for o in range(orbs)
         ]
-    for copy in outs:
-        copy.start()
-    for copy in outs:
-        copy.wait()
+        for copy in outs:
+            copy.start()
+        for copy in outs:
+            copy.wait()
 
 
 def filter_call(first, frag, shape, source, pot, band, previous):
@@ -188,9 +205,10 @@
             operands.append(previous)
             aliases = {3: 0}
     wide = 2 * plane + 2 * NB
+    dens = jax.ShapeDtypeStruct((pot.shape[0], pot.shape[2], plane), jnp.float32)
     return pl.pallas_call(
         body,
-        out_shape=(out, jax.ShapeDtypeStruct((side, plane), jnp.float32)),
+        out_shape=(out, dens),
         in_specs=in_specs,
         out_specs=(hbm, vmem),
         input_output_aliases=aliases,
@@ -231,49 +249,53 @@
     frag_count = orbitals.shape[0]
     block_count = potential.shape[0]
     piece_cells = potential.shape[1]
+    width = min(plane, piece_cells)
+    parts = plane // width
     capacity = CAP
     band = band_weights(side)
     entries, owners, ranks = owner_tables(frag_blocks, block_count, groups)
     count = entries.shape[1]
     slot_range = jnp.arange(capacity, dtype=jnp.int32)
     send_match = (owners[:, None, :] == me_index) & (ranks[:, None, :] == slot_range[None, :, None])
-    send_valid = jnp.any(send_match, axis=2).reshape(-1)
     send_block = jnp.sum(
         jnp.where(send_match, entries[:, None, :] - me_index * block_count, 0), axis=2
     ).reshape(-1)
-    send_mask = send_valid.astype(jnp.float32)[:, None]
     my_owners = lax.dynamic_index_in_dim(owners, me_index, 0, keepdims=False)
     my_ranks = lax.dynamic_index_in_dim(ranks, me_index, 0, keepdims=False)
+    my_entries = lax.dynamic_index_in_dim(entries, me_index, 0, keepdims=False)
     my_slot = my_owners * capacity + my_ranks
-    owner_range = jnp.arange(groups, dtype=jnp.int32)
-    back_match = (my_owners[None, None, :] == owner_range[:, None, None]) & (
-        my_ranks[None, None, :] == slot_range[None, :, None]
-    )
-    back_mask = jnp.any(back_match, axis=2).reshape(-1).astype(jnp.float32)[:, None]
-    entry_range = jnp.arange(count, dtype=jnp.int32)
-    back_entry = jnp.sum(jnp.where(back_match, entry_range[None, None, :], 0), axis=2).reshape(-1)
-    my_signs = jnp.repeat(
-        lax.dynamic_slice_in_dim(frag_signs, me_index * frag_count, frag_count), FB
-    ).astype(jnp.float32)
-    block_range = jnp.arange(block_count, dtype=jnp.int32)
-    selector = ((send_block[None, :] == block_range[:, None]) & send_valid[None, :]).astype(
-        jnp.float32
-    )
-    current_pot = potential
+    all_entries = entries.reshape(-1)
+    weights = jnp.repeat(frag_signs, FB).astype(jnp.float32) / ORBS
+    my_select = jnp.where(my_entries[:, None] == all_entries[None, :], weights[None, :], 0.0)
+    block_range = jnp.arange(block_count, dtype=jnp.int32) + me_index * block_count
+    owner_select = jnp.where(block_range[:, None] == all_entries[None, :], weights[None, :], 0.0)
+
+    every = lax.all_gather(potential, "frag", axis=0, tiled=True)
+    section = jnp.take(every, my_entries, axis=0)
+    owned = jnp.concatenate([ion_potential, core_density], axis=1)
+    outgoing = jnp.take(owned, send_block, axis=0).reshape(groups, capacity, 2 * piece_cells)
+    incoming = lax.all_to_all(outgoing, "frag", split_axis=0, concat_axis=0, tiled=True)
+    named = jnp.take(incoming.reshape(groups * capacity, -1), my_slot, axis=0)
+
+    def exchange(base, core, select, gathered):
+        collected = jnp.dot(
+            select,
+            gathered,
+            precision=lax.Precision.HIGHEST,
+            preferred_element_type=jnp.float32,
+        )
+        return base - EXCHANGE_COEF * jnp.cbrt(jnp.maximum(core + collected, DENSITY_FLOOR))
+
     middle = None
     filtered = None
     for iteration in range(ITERS):
-        outgoing = (jnp.take(current_pot, send_block, axis=0) * send_mask).reshape(
-            groups, capacity, piece_cells
-        )
-        incoming = lax.all_to_all(outgoing, "frag", split_axis=0, concat_axis=0, tiled=True)
-        sectioned = jnp.take(
-            incoming.reshape(groups * capacity, piece_cells), my_slot, axis=0
-        ).reshape(frag_count, FB, piece_cells)
+        pot = lax.all_gather(section.reshape(frag_count, -1, width), "orb", axis=0)
+        if parts > 1:
+            pot = pot.reshape(-1, parts, frag_count, FB, width)
+            pot = pot.transpose(0, 2, 3, 1, 4).reshape(-1, frag_count, FB, plane)
         pieces = []
         next_middle = []
         for frag in range(frag_count):
-            pot = lax.all_gather(sectioned[frag], "orb", axis=1, tiled=True).reshape(side, plane)
             if iteration == 0:
                 result, dens = filter_call(True, frag, orbitals.shape, orbitals, pot, band, None)
                 next_middle.append(result)
@@ -281,25 +303,25 @@
                 filtered, dens = filter_call(
                     False, frag, orbitals.shape, middle[frag], pot, band, filtered
                 )
-            pieces.append(
-                lax.psum_scatter(dens.reshape(FB, -1), "orb", scatter_dimension=1, tiled=True)
+            if parts > 1:
+                dens = dens.reshape(-1, FB, parts, width)
+                dens = dens.transpose(0, 2, 1, 3).reshape(-1, FB, width)
+            if iteration == 0:
+                dens = lax.all_to_all(dens, "orb", split_axis=0, concat_axis=0, tiled=True)
+                dens = jnp.sum(dens, axis=0)
+            pieces.append(dens)
+        if iteration > 0:
+            joined = jnp.concatenate(pieces, axis=1)
+            joined = lax.all_to_all(joined, "orb", split_axis=0, concat_axis=0, tiled=True)
+            pieces = [jnp.sum(joined, axis=0)]
+        middle = next_middle
+        summed = jnp.concatenate(pieces).reshape(count, piece_cells)
+        gathered = lax.all_gather(summed, "frag", axis=0, tiled=True)
+        if iteration + 1 < ITERS:
+            section = exchange(
+                named[:, :piece_cells], named[:, piece_cells:], my_select, gathered
             )
-        middle = next_middle
-        summed = jnp.stack(pieces)
-        signed = (summed / ORBS).reshape(count, piece_cells) * my_signs[:, None]
-        returning = (jnp.take(signed, back_entry, axis=0) * back_mask).reshape(
-            groups, capacity, piece_cells
-        )
-        arrived = lax.all_to_all(returning, "frag", split_axis=0, concat_axis=0, tiled=True)
-        collected = jnp.dot(
-            selector,
-            arrived.reshape(groups * capacity, piece_cells),
-            precision=lax.Precision.HIGHEST,
-            preferred_element_type=jnp.float32,
-        )
-        total = core_density + collected
-        current_pot = ion_potential - EXCHANGE_COEF * jnp.cbrt(jnp.maximum(total, DENSITY_FLOOR))
-    return (filtered, current_pot)
+    return (filtered, exchange(ion_potential, core_density, owner_select, gathered))
 
 
 def solution(mesh):

time: 978 us -> 308 us (0.31)
  waiting for transfers between devices: 654 us -> 60.7 us
  local copies, waits for them, and re-layouts: 61.3 us -> 6.38 us
  blocking collectives: 88.4 us -> 67.9 us
  between operations: 14.1 us -> 0.96 us
  starting transfers between devices: 5.69 us -> 16.3 us
    unnamed x8 -> x0, waiting for transfers between devices: 648 us -> none
    all_to_all x0 -> x3, waiting for transfers between devices: none -> 60.7 us  [the longest x2 31.3 us: shards(): dens = lax.all_to_all(dens, 'orb', split_axis=0, concat_axis=0, tiled=True)]
    unnamed x26 -> x18, local copies, waits for them, and re-layouts: 51.9 us -> 2.3 us
    all_to_all x3 -> x0, blocking collectives: 27.8 us -> none  [the longest x2 19.2 us: shards(): lax.all_to_all(returning, 'frag', split_axis=0, concat_axis=0, tiled=True)]
    all_to_all x0 -> x3, starting transfers between devices: none -> 11.1 us  [the longest x2 7.56 us: shards(): dens = lax.all_to_all(dens, 'orb', split_axis=0, concat_axis=0, tiled=True)]
    all_gather x4 -> x5, blocking collectives: 60.6 us -> 67.9 us  [the longest x2 33 us: shards(): pot = lax.all_gather(section.reshape(frag_count, -1, width), 'orb', axis=0)]
  transfers between devices with their start and end apart: 5 -> 4, of which waited for: 5 -> 3; matrix products, arithmetic and copies ran while one was open for 3% -> 1% of each run, Pallas kernels for 8% -> 24%
where the time goes in v2:
time: 308 us; the launch traced here: 307 us
  Pallas kernels  148 us (48%)
  blocking collectives  67.9 us (22%)
  waiting for transfers between devices  60.7 us (20%)
  starting transfers between devices  16.3 us (5%)
  local copies, waits for them, and re-layouts  6.38 us (2%)
  other arithmetic  4.97 us (2%)
    pallas_call x4, Pallas kernels, filter_call(): pl.pallas_call(body, out_shape=(out, dens), in_specs=in_specs, out_specs=...  148 us
    all_gather x2, blocking collectives, shards(): pot = lax.all_gather(section.reshape(frag_count, -1, width), 'orb', axis=0)  33 us
    all_to_all x2, waiting for transfers between devices, shards(): dens = lax.all_to_all(dens, 'orb', split_axis=0, concat_axis=0, tiled=True)  31.3 us
    all_to_all x1, waiting for transfers between devices, shards(): lax.all_to_all(joined, 'orb', split_axis=0, concat_axis=0, tiled=True)  29.3 us
    all_gather x2, blocking collectives, shards(): gathered = lax.all_gather(summed, 'frag', axis=0, tiled=True)  20.3 us
    all_gather x1, blocking collectives, shards(): every = lax.all_gather(potential, 'frag', axis=0, tiled=True)  14.6 us
    all_to_all x2, starting transfers between devices, shards(): dens = lax.all_to_all(dens, 'orb', split_axis=0, concat_axis=0, tiled=True)  7.56 us
  transfers between devices with their start and end apart: 4, of which 3 were waited for; matrix products, arithmetic and copies ran while one was open for 1% of the time, Pallas kernels for 24%

profile of v2, /device:TPU:0, one launch (start us, length us, event | category | flops | bytes accessed | tf_op | source)
XLA Modules:
  0.0 307.1 jit_solution(12054443281095034599)
XLA Ops:
  0.6 0.8 copy.38
  2.6 1.0 pad_maximum_fusion.1
  3.6 0.7 gather_fusion.1
  4.6 1.0 broadcast_select_fusion
  5.6 5.2 %all-to-all-start = ((f32[4,3,9216]{2,1,0:T(4,128)}), f32[4,3,9216]{2,1,0:T(4,128)S(1)}, u32[]{:S(2)}, u32[]{:S(2)}) async-start(f32[4,3,9216]{2,1,0:T(4,128)} %broadcast_select_fusion), calls=%async_computation | async-start | bytes 1179648 | tf_op jit(solution)/shard_map/all_to_all | solution.py:277
  11.1 14.6 %all-gather = f32[4,6,4608]{2,1,0:T(8,128)S(1)} all-gather(f32[1,6,4608]{2,1,0:T(8,128)S(1)} %bitcast.15), channel_id=1, replica_groups=mesh['frag'=4,'orb'=8] {'frag'}, dimensions={0}, use_global_device_ids=true | all-gather | bytes 552960 | tf_op jit(solution)/shard_map/all_gather | solution.py:273
  26.5 16.8 %all_gather.16 = f32[8,2,6,2304]{3,1,2,0:T(2,128)S(1)} all-gather(f32[1,2,6,2304]{3,1,2,0:T(2,128)S(1)} %copy.39), channel_id=1, replica_groups=mesh['frag'=4,'orb'=8] {'orb'}, dimensions={0}, use_global_device_ids=true | all-gather | bytes 995328 | tf_op jit(solution)/shard_map/all_gather | solution.py:292
  43.5 1.3 copy-done
  44.7 36.8 %filter_fragment.5 = (f32[48,16,2304]{2,1,0:T(8,128)}, f32[8,6,2304]{2,1,0:T(8,128)}) custom-call(f32[2,16,48,2304]{3,2,1,0:T(8,128)} %refs_0_.3, f32[8,2,6,2304]{3,2,1,0:T(8,128)S(1)} %copy.40.refs_1_, bf16[3,1024,256]{2,1,0:T(8,128)(2,1)S(1)} %copy-done), custom_call_target="tpu_custom_call" | custom-call | flops 14495514624 | bytes 14155776 | tf_op jit(solution)/shard_map/filter_fragment/pallas_call | solution.py:209
  81.5 36.8 %filter_fragment.4 = (f32[48,16,2304]{2,1,0:T(8,128)}, f32[8,6,2304]{2,1,0:T(8,128)}) custom-call(f32[2,16,48,2304]{3,2,1,0:T(8,128)} %refs_0_.3, f32[8,2,6,2304]{3,2,1,0:T(8,128)S(1)} %copy.40.refs_1_, bf16[3,1024,256]{2,1,0:T(8,128)(2,1)S(1)} %copy-done), custom_call_target="tpu_custom_call" | custom-call | flops 14495514624 | bytes 14155776 | tf_op jit(solution)/shard_map/filter_fragment/pallas_call | solution.py:209
  118.5 4.0 %all-to-all-start.1 = ((f32[8,6,2304]{2,1,0:T(8,128)}), f32[8,6,2304]{2,1,0:T(8,128)S(1)}, u32[]{:S(2)}, u32[]{:S(2)}) async-start(f32[8,6,2304]{2,1,0:T(8,128)} %get-tuple-element.11), calls=%async_computation.1 | async-start | bytes 1179648 | tf_op jit(solution)/shard_map/all_to_all | solution.py:310
  123.8 15.5 %all-to-all-done.1 = f32[8,6,2304]{2,1,0:T(8,128)S(1)} async-done(((f32[8,6,2304]{2,1,0:T(8,128)}), f32[8,6,2304]{2,1,0:T(8,128)S(1)}, u32[]{:S(2)}, u32[]{:S(2)}) %all-to-all-start.1) | async-done | bytes 442400 | tf_op jit(solution)/shard_map/all_to_all | solution.py:310
  139.3 3.5 %all-to-all-start.2 = ((f32[8,6,2304]{2,1,0:T(8,128)}), f32[8,6,2304]{2,1,0:T(8,128)S(1)}, u32[]{:S(2)}, u32[]{:S(2)}) async-start(f32[8,6,2304]{2,1,0:T(8,128)} %get-tuple-element.12), calls=%async_computation.2 | async-start | bytes 1179648 | tf_op jit(solution)/shard_map/all_to_all | solution.py:310
  142.8 0.8 broadcast_select_fusion.1
  143.7 15.8 %all-to-all-done.2 = f32[8,6,2304]{2,1,0:T(8,128)S(1)} async-done(((f32[8,6,2304]{2,1,0:T(8,128)}), f32[8,6,2304]{2,1,0:T(8,128)S(1)}, u32[]{:S(2)}, u32[]{:S(2)}) %all-to-all-start.2) | async-done | bytes 442400 | tf_op jit(solution)/shard_map/all_to_all | solution.py:310
  159.6 9.4 %all-gather.1 = f32[4,6,4608]{2,1,0:T(8,128)S(1)} all-gather(f32[1,6,4608]{2,1,0:T(8,128)S(1)} %reshape.267), channel_id=1, replica_groups=mesh['frag'=4,'orb'=8] {'frag'}, dimensions={0}, use_global_device_ids=true | all-gather | bytes 552960 | tf_op jit(solution)/shard_map/all_gather | solution.py:319
  169.7 16.2 %all_gather.18 = f32[8,2,6,2304]{3,1,2,0:T(2,128)S(1)} all-gather(f32[1,2,6,2304]{3,1,2,0:T(2,128)S(1)} %copy.51), channel_id=1, replica_groups=mesh['frag'=4,'orb'=8] {'orb'}, dimensions={0}, use_global_device_ids=true | all-gather | bytes 995328 | tf_op jit(solution)/shard_map/all_gather | solution.py:292
  186.1 37.3 %filter_fragment.6 = (f32[2,16,48,2304]{3,2,1,0:T(8,128)}, f32[8,6,2304]{2,1,0:T(8,128)S(1)}) custom-call(f32[48,16,2304]{2,1,0:T(8,128)} %get-tuple-element.13.refs_0_, f32[8,2,6,2304]{3,2,1,0:T(8,128)S(1)} %copy.53.refs_1_, bf16[3,1024,256]{2,1,0:T(8,128)(2,1)S(1)} %copy-done), custom_call_target="tpu_custom_call" | custom-call | flops 14495514624 | bytes 14155776 | tf_op jit(solution)/shard_map/filter_fragment/pallas_call | solution.py:209
  223.4 37.4 %filter_fragment.7 = (f32[2,16,48,2304]{3,2,1,0:T(8,128)}, f32[8,6,2304]{2,1,0:T(8,128)S(1)}) custom-call(f32[48,16,2304]{2,1,0:T(8,128)} %get-tuple-element.10.refs_0_, f32[8,2,6,2304]{3,2,1,0:T(8,128)S(1)} %copy.53.refs_1_, bf16[3,1024,256]{2,1,0:T(8,128)(2,1)S(1)} %copy-done, ...), custom_call_target="tpu_custom_call", output_to_operand_aliasing={{0}: (3, {})} | custom-call | flops 14495514624 | bytes 14155776 | tf_op jit(solution)/shard_map/filter_fragment/pallas_call | solution.py:209
  260.8 1.2 pad_maximum_fusion
  261.9 3.6 %all-to-all-start.3 = ((f32[8,12,2304]{2,1,0:T(8,128)}), f32[8,12,2304]{2,1,0:T(8,128)S(1)}, u32[]{:S(2)}, u32[]{:S(2)}) async-start(f32[8,12,2304]{2,1,0:T(8,128)} %pad_maximum_fusion), calls=%async_computation.3 | async-start | bytes 2359296 | tf_op jit(solution)/shard_map/all_to_all | solution.py:315
  265.5 29.3 %all-to-all-done.3 = f32[8,12,2304]{2,1,0:T(8,128)S(1)} async-done(((f32[8,12,2304]{2,1,0:T(8,128)}), f32[8,12,2304]{2,1,0:T(8,128)S(1)}, u32[]{:S(2)}, u32[]{:S(2)}) %all-to-all-start.3) | async-done | bytes 884768 | tf_op jit(solution)/shard_map/all_to_all | solution.py:315
  295.0 10.9 %all-gather.2 = f32[4,6,4608]{2,1,0:T(8,128)S(1)} all-gather(f32[1,6,4608]{2,1,0:T(8,128)S(1)} %reshape.269), channel_id=1, replica_groups=mesh['frag'=4,'orb'=8] {'frag'}, dimensions={0}, use_global_device_ids=true | all-gather | bytes 552960 | tf_op jit(solution)/shard_map/all_gather | solution.py:319
  306.0 1.2 fusion.7
  (65 shorter events, 5.1 us)
Async XLA Ops:
  4.6 6.5 %copy-start.4 = (f32[6,4608]{1,0:T(8,128)S(1)}, f32[6,4608]{1,0:T(8,128)}, u32[]{:S(2)}) copy-start(f32[6,4608]{1,0:T(8,128)} %param.8) | copy-start | bytes 331780
  5.6 112.9 %all-to-all-start = ((f32[4,3,9216]{2,1,0:T(4,128)}), f32[4,3,9216]{2,1,0:T(4,128)S(1)}, u32[]{:S(2)}, u32[]{:S(2)}) async-start(f32[4,3,9216]{2,1,0:T(4,128)} %broadcast_select_fusion), calls=%async_computation | async-start | bytes 1179648 | tf_op jit(solution)/shard_map/all_to_all | solution.py:277
  43.3 1.4 copy-start
  118.4 4.1 %copy-start.5 = (s32[8]{0:T(128)S(1)}, s32[8]{0:T(128)}, u32[]{:S(2)}) copy-start(s32[8]{0:T(128)} %param.12) | copy-start | bytes 100
  118.5 20.8 %all-to-all-start.1 = ((f32[8,6,2304]{2,1,0:T(8,128)}), f32[8,6,2304]{2,1,0:T(8,128)S(1)}, u32[]{:S(2)}, u32[]{:S(2)}) async-start(f32[8,6,2304]{2,1,0:T(8,128)} %get-tuple-element.11), calls=%async_computation.1 | async-start | bytes 1179648 | tf_op jit(solution)/shard_map/all_to_all | solution.py:310
  139.3 20.2 %all-to-all-start.2 = ((f32[8,6,2304]{2,1,0:T(8,128)}), f32[8,6,2304]{2,1,0:T(8,128)S(1)}, u32[]{:S(2)}, u32[]{:S(2)}) async-start(f32[8,6,2304]{2,1,0:T(8,128)} %get-tuple-element.12), calls=%async_computation.2 | async-start | bytes 1179648 | tf_op jit(solution)/shard_map/all_to_all | solution.py:310
  159.5 9.5 %copy-start.1 = (f32[6,9216]{1,0:T(8,128)S(1)}, f32[6,9216]{1,0:T(8,128)}, u32[]{:S(2)}) copy-start(f32[6,9216]{1,0:T(8,128)} %broadcast_select_fusion.1) | copy-start | bytes 663556
  261.9 32.9 %all-to-all-start.3 = ((f32[8,12,2304]{2,1,0:T(8,128)}), f32[8,12,2304]{2,1,0:T(8,128)S(1)}, u32[]{:S(2)}, u32[]{:S(2)}) async-start(f32[8,12,2304]{2,1,0:T(8,128)} %pad_maximum_fusion), calls=%async_computation.3 | async-start | bytes 2359296 | tf_op jit(solution)/shard_map/all_to_all | solution.py:315
  294.9 11.0 %copy-start.2 = (f32[6,4608]{1,0:T(8,128)S(1)}, f32[6,4608]{1,0:T(8,128)}, u32[]{:S(2)}) copy-start(f32[6,4608]{1,0:T(8,128)} %param.10) | copy-start | bytes 331780
  294.9 11.0 %copy-start.3 = (f32[6,4608]{1,0:T(8,128)S(1)}, f32[6,4608]{1,0:T(8,128)}, u32[]{:S(2)}) copy-start(f32[6,4608]{1,0:T(8,128)} %param.9) | copy-start | bytes 331780
